TPU v7x, 512 devices: a whole 4x4x16 slice. The times are simulated.
512 devices in a mesh: dp: 64 (over y, x, z_hi, core), mp: 8 (over z_lo).
Axes of the slice: x: 4, y: 4, z: 16 (z_hi: 2, z_lo: 8; z = z_hi * 8 + z_lo), core: 2. Of those that a mesh axis runs over, the one named last changes fastest.
Arguments:
- activations: bfloat16 [8192, 4096], P('dp', 'mp'), may hold values from -27 to 27
- out_grads: bfloat16 [8192, 8192], P('dp', 'mp'), may hold values from -27 to 27
- grad_weight: bfloat16 [8192, 4096], P('mp', 'dp'), may hold values from -6 to 6
- basis_a: bfloat16 [4096, 512], P('mp'), may hold values from -0.25 to 0.25
- basis_g: bfloat16 [8192, 512], P('mp'), may hold values from -0.25 to 0.25
Outputs:
- factor_a: float32 [4096, 512], P(('mp', 'dp'))
- factor_g: float32 [8192, 512], P(('mp', 'dp'))
- precond: float32 [8192, 4096], P('mp', 'dp')
All inputs are finite; a program needn't handle non-finite values.
Results may differ from a plain program's by a relative error of at most 0.0065.
Values may be sent and summed in bfloat16 or wider, within the bound.
A program may use at most 64 MiB of HBM per device.

v0:
```python
import jax
import jax.numpy as jnp
from jax import lax
from jax.sharding import PartitionSpec as P

damping = 0.01


def block_covariance(values, block_size, tokens):
    count = values.shape[1] // block_size
    shaped = values.reshape(values.shape[0], count, block_size)
    product = jnp.einsum("tbr,tbs->brs", shaped, shaped, preferred_element_type=jnp.float32)
    return product.reshape(count * block_size, block_size) / tokens


def whole_diagonal(factor, basis, block_size):
    count = factor.shape[0] // block_size
    factor_blocks = factor.reshape(count, block_size, block_size)
    basis_blocks = basis.astype(jnp.float32).reshape(count, block_size, block_size)
    product = jnp.einsum(
        "nrs,nsc->nrc", factor_blocks, basis_blocks, precision=lax.Precision.HIGHEST
    )
    return jnp.sum(basis_blocks * product, axis=1).reshape(-1)


def shards(activations, out_grads, grad_weight, basis_a, basis_g):
    replicas = lax.axis_size("dp")
    dp_index = lax.axis_index("dp")
    block_size = basis_a.shape[1]
    tokens = activations.shape[0] * replicas
    count_g = basis_g.shape[0] // block_size
    grad_cols = grad_weight.shape[1]
    local_rows = basis_g.shape[0]
    left_basis = basis_g.reshape(count_g, block_size, block_size)
    grad_blocks = grad_weight.reshape(count_g, block_size, grad_cols)
    left = jnp.einsum("brs,brd->bsd", left_basis, grad_blocks, preferred_element_type=jnp.float32)
    left = left.astype(jnp.bfloat16).reshape(local_rows, grad_cols)
    part_a = block_covariance(activations, block_size, tokens)
    part_g = block_covariance(out_grads, block_size, tokens)
    rows_a = part_a.shape[0] // replicas
    rows_g = part_g.shape[0] // replicas
    summed_a, summed_g = lax.psum((part_a, part_g), "dp")
    diag_a = whole_diagonal(summed_a, basis_a, block_size)
    diag_g = whole_diagonal(summed_g, basis_g, block_size)
    share_a = lax.dynamic_slice_in_dim(summed_a, dp_index * rows_a, rows_a, 0)
    share_g = lax.dynamic_slice_in_dim(summed_g, dp_index * rows_g, rows_g, 0)
    spread = lax.all_to_all(left, "dp", split_axis=0, concat_axis=1, tiled=True)
    full_basis = lax.all_gather(basis_a, "mp", axis=0, tiled=True)
    columns_diag = lax.all_gather(diag_a, "mp", axis=0, tiled=True)
    spread_rows = spread.shape[0]
    row_diag = lax.dynamic_slice_in_dim(diag_g, dp_index * spread_rows, spread_rows, 0)
    count_a = full_basis.shape[0] // block_size
    right_basis = full_basis.reshape(count_a, block_size, block_size)
    rotated = jnp.einsum(
        "rbs,bsc->rbc",
        spread.reshape(spread_rows, count_a, block_size),
        right_basis,
        preferred_element_type=jnp.float32,
    )
    divisor = row_diag[:, None, None] * columns_diag.reshape(1, count_a, block_size) + damping
    scaled = (rotated / divisor).astype(jnp.bfloat16)
    back = jnp.einsum("rbc,bsc->rbs", scaled, right_basis, preferred_element_type=jnp.float32)
    back = back.astype(jnp.bfloat16).reshape(spread_rows, count_a * block_size)
    returned = lax.all_to_all(back, "dp", split_axis=1, concat_axis=0, tiled=True)
    precond = jnp.einsum(
        "brs,bsd->brd",
        left_basis,
        returned.reshape(count_g, block_size, grad_cols),
        preferred_element_type=jnp.float32,
    )
    return (share_a, share_g, precond.reshape(local_rows, grad_cols))


def solution(mesh):
    in_specs = (P("dp", "mp"), P("dp", "mp"), P("mp", "dp"), P("mp", None), P("mp", None))
    out_specs = (P(("mp", "dp"), None), P(("mp", "dp"), None), P("mp", "dp"))
    return jax.shard_map(shards, mesh=mesh, in_specs=in_specs, out_specs=out_specs, check_vma=False)
```

profile of v0, /device:TPU:1, one launch (start us, length us, event | category | flops | bytes accessed | tf_op | source)
XLA Modules:
  0.0 1254.2 jit_solution(946190482016432474)
XLA Ops:
  8.1 2.9 convolution_multiply_fusion
  11.0 1.3 convolution_multiply_fusion.2
  12.3 0.5 all-gather.3.cloned.1.call-update
  12.8 0.6 copy-done.1
  13.5 0.3 convolution_convert_fusion.1
  13.9 0.8 reshape.88
  14.8 22.2 %all-to-all-start = ((bf16[64,2,512]{2,1,0:T(2,128)(2,1)}), bf16[64,2,512]{2,1,0:T(2,128)(2,1)S(1)}, u32[]{:S(2)}, u32[]{:S(2)}) async-start(bf16[64,2,512]{2,1,0:T(2,128)(2,1)} %reshape.88), calls=%async_computation | async-start | bytes 262144 | tf_op jit(solution)/shard_map/all_to_all | solution.py:47
  37.0 20.6 %all-to-all-done = bf16[64,2,512]{2,1,0:T(2,128)(2,1)S(1)} async-done(((bf16[64,2,512]{2,1,0:T(2,128)(2,1)}), bf16[64,2,512]{2,1,0:T(2,128)(2,1)S(1)}, u32[]{:S(2)}, u32[]{:S(2)}) %all-to-all-start) | async-done | bytes 131104 | tf_op jit(solution)/shard_map/all_to_all | solution.py:47
  57.7 0.2 reshape.89
  58.0 0.2 reshape.77
  58.2 1099.1 %all-reduce.3.cloned.1.call-done = (f32[512,512]{1,0:T(8,128)}, f32[1024,512]{1,0:T(8,128)}) async-done(((f32[512,512]{1,0:T(8,128)}, f32[1024,512]{1,0:T(8,128)}), (f32[512,512]{1,0:T(8,128)}, f32[1024,512]{1,0:T(8,128)})) %all-reduce.3.cloned.1.call-update) | async-done | bytes 3145744 | tf_op jit(solution)/shard_map/psum | solution.py:42
  1157.3 3.5 multiply_reduce_fusion
  1160.8 1.0 fusion
  1161.8 37.1 %all-gather = f32[8,1,512]{2,1,0:T(1,128)S(1)} all-gather(f32[1,1,512]{2,1,0:T(1,128)S(1)} %bitcast.65), channel_id=1, replica_groups=mesh['dp'=64,'mp'=8] {'mp'}, dimensions={0}, use_global_device_ids=true | all-gather | bytes 18432 | tf_op jit(solution)/shard_map/all_gather | solution.py:49
  1198.9 5.2 fusion.3
  1204.2 0.2 all_to_all.27
  1204.6 0.8 reshape.90
  1205.5 22.6 %all-to-all-start.1 = ((bf16[64,2,512]{2,1,0:T(2,128)(2,1)}), bf16[64,2,512]{2,1,0:T(2,128)(2,1)S(1)}, u32[]{:S(2)}, u32[]{:S(2)}) async-start(bf16[64,2,512]{2,1,0:T(2,128)(2,1)} %reshape.90), calls=%async_computation.1 | async-start | bytes 262144 | tf_op jit(solution)/shard_map/all_to_all | solution.py:64
  1228.1 0.6 constant_dynamic-slice_fusion.1
  1228.7 1.4 constant_dynamic-slice_fusion
  1230.1 15.2 %all-to-all-done.1 = bf16[64,2,512]{2,1,0:T(2,128)(2,1)S(1)} async-done(((bf16[64,2,512]{2,1,0:T(2,128)(2,1)}), bf16[64,2,512]{2,1,0:T(2,128)(2,1)S(1)}, u32[]{:S(2)}, u32[]{:S(2)}) %all-to-all-start.1) | async-done | bytes 131104 | tf_op jit(solution)/shard_map/all_to_all | solution.py:64
  1245.4 0.2 reshape.91
  1245.6 0.4 convolution_bitcast_fusion.1
  1246.0 0.7 copy.34
  (20 shorter events, 0.7 us)
Async XLA Ops:
  8.0 3.0 copy-start
  8.0 1149.2 %all-reduce.3.cloned.1.call-start = ((), (), s32[]{:S(2)}) async-start(), calls=%async_computation.3 | async-start | bytes 6291456 | tf_op jit(solution)/shard_map/psum | solution.py:42
  12.2 1.2 copy-start.1
  12.2 1.2 copy-start.4
  12.3 1186.7 %all-gather.3.cloned.1.call-start = ((), (), s32[]{:S(2)}) async-start(), calls=%async_computation.2 | async-start | bytes 4718592 | tf_op jit(solution)/shard_map/all_gather | solution.py:48
  14.8 42.9 %all-to-all-start = ((bf16[64,2,512]{2,1,0:T(2,128)(2,1)}), bf16[64,2,512]{2,1,0:T(2,128)(2,1)S(1)}, u32[]{:S(2)}, u32[]{:S(2)}) async-start(bf16[64,2,512]{2,1,0:T(2,128)(2,1)} %reshape.88), calls=%async_computation | async-start | bytes 262144 | tf_op jit(solution)/shard_map/all_to_all | solution.py:47
  57.9 1102.9 %copy-start.2 = (bf16[512,512]{1,0:T(8,128)(2,1)S(1)}, bf16[512,512]{1,0:T(8,128)(2,1)}, u32[]{:S(2)}) copy-start(bf16[512,512]{1,0:T(8,128)(2,1)} %param.8) | copy-start | bytes 1572868
  1157.2 3.5 copy-start.3
  1205.5 39.9 %all-to-all-start.1 = ((bf16[64,2,512]{2,1,0:T(2,128)(2,1)}), bf16[64,2,512]{2,1,0:T(2,128)(2,1)S(1)}, u32[]{:S(2)}, u32[]{:S(2)}) async-start(bf16[64,2,512]{2,1,0:T(2,128)(2,1)} %reshape.90), calls=%async_computation.1 | async-start | bytes 262144 | tf_op jit(solution)/shard_map/all_to_all | solution.py:64
Sparse Core Ops, SparseCore 0:
  12.4 1144.8 all-reduce.2
Sparse Core Ops, SparseCore 1:
  15.0 127.2 all-gather.2
where the time goes:
time: 1250 us
  waiting for transfers between devices  1140 us (91%)
  starting transfers between devices  45 us (4%)
  blocking collectives  37.1 us (3%)
  between operations  15.6 us (1%)
  matrix products  14.6 us (1%)
    psum x1, waiting for transfers between devices, shards(): summed_a, summed_g = lax.psum((part_a, part_g), 'dp')  1100 us
    all_gather x1, blocking collectives, shards(): columns_diag = lax.all_gather(diag_a, 'mp', axis=0, tiled=True)  37.1 us
  transfers between devices with their start and end apart: 4, of which 3 were waited for; matrix products, arithmetic and copies ran while one was open for 1% of the time, Pallas kernels for 0%

commit v1 on v0

v1 whole, which is shorter than its diff:
```python
import functools

import jax
import jax.numpy as jnp
from jax import lax
from jax.experimental import pallas as pl
from jax.experimental.pallas import tpu as pltpu
from jax.sharding import PartitionSpec as P

MESH = pl.DeviceIdType.MESH
damping = 0.01
CHUNKS = 8


def dot(a, b, dim_a, dim_b):
    return lax.dot_general(a, b, (((dim_a,), (dim_b,)), ((), ())), preferred_element_type=jnp.float32)


def row_picker(size, group, core):
    row = lax.broadcasted_iota(jnp.int32, (size, size // 2), 0)
    col = lax.broadcasted_iota(jnp.int32, (size, size // 2), 1)
    within = lax.rem(col, group)
    return jnp.where(row == (col - within) * 2 + group * core + within, 1.0, 0.0).astype(jnp.bfloat16)


def kernel(
    ny, nx, tokens,
    xa_in, xg_in, w_in, qa_in, pg_in,
    oa_out, og_out, op_out,
    xa, xg, w, qa, pg,
    lsend, lrecv, bsend, brecv,
    dsend, drecv, dzsend, dzrecv, gsend, grecv,
    fsend, frecv, fsum, fzsend, fzrecv,
    oa, og, op,
    load_sem, core_send, core_recv,
    lsend_sem, lrecv_sem, bsend_sem, brecv_sem,
    dsend_sem, drecv_sem, dz_sem, gsend_sem, grecv_sem,
    fsend_sem, frecv_sem, fz_sem, out_sem,
):
    d = lax.axis_index("dp")
    m = lax.axis_index("mp")
    core = lax.rem(d, 2)
    zh = lax.rem(d // 2, 2)
    place = d // 4
    x = lax.rem(place, nx)
    y = place // nx
    places = ny * nx
    group = d // CHUNKS
    lane = lax.rem(d, CHUNKS)
    diagonal = group == m
    rows_a, rows_g = oa.shape[0], og.shape[0]
    block = qa.shape[0]
    cols = w.shape[0]

    twin = (d + 1 - 2 * core, m)
    across = (d + 2 - 4 * zh, m)

    def peer(step, sign):
        dy, dx = step // nx, lax.rem(step, nx)
        to_y = lax.rem(y + sign * dy + ny, ny)
        to_x = lax.rem(x + sign * dx + nx, nx)
        return to_y * nx + to_x

    def at_place(p):
        return (p * 4 + zh * 2 + core, m)

    def friend(q):
        return (m * CHUNKS + q, group)

    def is_me(q):
        return jnp.logical_and(diagonal, q == lane)

    loads = [
        pltpu.make_async_copy(src, dst, load_sem.at[i])
        for i, (src, dst) in enumerate(
            ((w_in, w), (pg_in, pg), (xa_in, xa.at[0]), (xg_in, xg.at[0]), (qa_in, qa))
        )
    ]
    for load in loads:
        load.start()

    barrier = pltpu.get_barrier_semaphore()

    def greet(device):
        pl.semaphore_signal(barrier, inc=1, device_id=device, device_id_type=MESH)

    greet(twin)
    greet(across)

    @pl.loop(1, places)
    def _(step):
        greet(at_place(peer(step, 1)))

    @pl.loop(0, CHUNKS)
    def _(q):
        @pl.when(jnp.logical_not(is_me(q)))
        def _():
            greet(friend(q))

    pl.semaphore_wait(barrier, 2 + places - 1 + CHUNKS - diagonal.astype(jnp.int32))

    swap_a = pltpu.make_async_remote_copy(
        src_ref=xa_in, dst_ref=xa.at[1], send_sem=core_send.at[0], recv_sem=core_recv.at[0],
        device_id=twin, device_id_type=MESH,
    )
    swap_g = pltpu.make_async_remote_copy(
        src_ref=xg_in, dst_ref=xg.at[1], send_sem=core_send.at[1], recv_sem=core_recv.at[1],
        device_id=twin, device_id_type=MESH,
    )
    swap_a.start()
    swap_g.start()

    loads[0].wait()
    loads[1].wait()
    per_block = block // lsend.shape[2]
    for b in range(pg.shape[0] // block):
        left = dot(w[:, b * block:(b + 1) * block], pg[b * block:(b + 1) * block, :], 1, 0)
        left = left.astype(jnp.bfloat16)
        for i in range(per_block):
            lsend[b * per_block + i] = left[:, i * lsend.shape[2]:(i + 1) * lsend.shape[2]]

    def left_copy(q, slot):
        return pltpu.make_async_remote_copy(
            src_ref=lsend.at[q], dst_ref=lrecv.at[slot],
            send_sem=lsend_sem.at[q], recv_sem=lrecv_sem.at[slot],
            device_id=friend(q), device_id_type=MESH,
        )

    def back_copy(q, slot):
        return pltpu.make_async_remote_copy(
            src_ref=bsend.at[q], dst_ref=brecv.at[slot],
            send_sem=bsend_sem.at[q], recv_sem=brecv_sem.at[slot],
            device_id=friend(q), device_id_type=MESH,
        )

    def send_all(copy, src, dst):
        @pl.loop(0, CHUNKS)
        def _(q):
            @pl.when(jnp.logical_not(is_me(q)))
            def _():
                copy(q, lane).start()

            @pl.when(is_me(q))
            def _():
                dst[pl.ds(q, 1)] = src[pl.ds(q, 1)]

    def receive_all(copy):
        @pl.loop(0, CHUNKS)
        def _(k):
            @pl.when(jnp.logical_not(is_me(k)))
            def _():
                copy(k, k).wait_recv()

    def drain_all(copy):
        @pl.loop(0, CHUNKS)
        def _(q):
            @pl.when(jnp.logical_not(is_me(q)))
            def _():
                copy(q, lane).wait_send()

    send_all(left_copy, lsend, lrecv)

    for load in loads[2:]:
        load.wait()
    swap_a.wait_recv()
    swap_g.wait_recv()
    xa_all = xa[...].reshape(-1, block)
    xg_all = [
        xg[:, :, b * block:(b + 1) * block].reshape(-1, block) for b in range(pg.shape[0] // block)
    ]
    half = block // 2
    sides = [(xa_all, qa[...])] + [
        (values, pg[b * block:(b + 1) * block, :]) for b, values in enumerate(xg_all)
    ]
    dsend[...] = jnp.zeros_like(dsend)
    for i, (values, basis) in enumerate(sides):
        turned = dot(values, basis, 1, 0)
        total = jnp.sum(turned * turned, axis=0, keepdims=True)
        dsend[2 * i:2 * i + 1, :] = total[:, :half]
        dsend[2 * i + 1:2 * i + 2, :] = total[:, half:]

    def diag_copy(step):
        return pltpu.make_async_remote_copy(
            src_ref=dsend, dst_ref=drecv.at[step],
            send_sem=dsend_sem.at[step], recv_sem=drecv_sem.at[step],
            device_id=at_place(peer(step, 1)), device_id_type=MESH,
        )

    @pl.loop(1, places)
    def _(step):
        diag_copy(step).start()

    pick_a = row_picker(block, rows_a, core)
    pick_g = row_picker(block, rows_g, core)
    picked = dot(xa_all, pick_a, 1, 0).astype(jnp.bfloat16)
    part = dot(picked, xa_all, 0, 0).astype(jnp.bfloat16)
    fsend[:, 0:2 * rows_a, :] = part.reshape(places, 2 * rows_a, block)
    each = places // len(xg_all)
    for b, values in enumerate(xg_all):
        picked = dot(values, pick_g, 1, 0).astype(jnp.bfloat16)
        part = dot(picked, values, 0, 0).astype(jnp.bfloat16)
        fsend[b * each:(b + 1) * each, 2 * rows_a:, :] = part.reshape(each, 2 * rows_g, block)

    def factor_copy(step):
        to = peer(step, 1)
        return pltpu.make_async_remote_copy(
            src_ref=fsend.at[to], dst_ref=frecv.at[step],
            send_sem=fsend_sem.at[step], recv_sem=frecv_sem.at[step],
            device_id=at_place(to), device_id_type=MESH,
        )

    @pl.loop(1, places)
    def _(step):
        factor_copy(step).start()

    drecv[0] = dsend[...]

    @pl.loop(1, places)
    def _(step):
        diag_copy(step).wait_recv()

    mine = jnp.sum(drecv[...], axis=0)
    dzsend[...] = mine
    for q in range(CHUNKS):
        r, c = 2 + q // 2, (q % 2) * 128
        gsend[q] = jnp.broadcast_to(mine[r:r + 1, c:c + 128], (8, 128))
    dz_copy = pltpu.make_async_remote_copy(
        src_ref=dzsend, dst_ref=dzrecv, send_sem=dz_sem.at[0], recv_sem=dz_sem.at[1],
        device_id=across, device_id_type=MESH,
    )
    dz_copy.start()

    def g_copy(q, slot):
        return pltpu.make_async_remote_copy(
            src_ref=gsend.at[q], dst_ref=grecv.at[slot],
            send_sem=gsend_sem.at[slot], recv_sem=grecv_sem.at[slot],
            device_id=friend(q), device_id_type=MESH,
        )

    other = lane + 2 - 4 * zh
    g_copy(other, 1).start()

    @pl.when(jnp.logical_not(diagonal))
    def _():
        g_copy(lane, 0).start()

    @pl.when(diagonal)
    def _():
        grecv[pl.ds(0, 1)] = gsend[pl.ds(lane, 1)]

    receive_all(left_copy)
    rows = lrecv.shape[2]
    rotated = dot(lrecv[...].reshape(block, rows), qa[...], 0, 0)

    dz_copy.wait_recv()
    g_copy(other, 1).wait_recv()

    @pl.when(jnp.logical_not(diagonal))
    def _():
        g_copy(lane, 0).wait_recv()

    both = (dzsend[0:2, :] + dzrecv[0:2, :]) * (1.0 / tokens)
    diag_a = jnp.concatenate([both[0:1, :], both[1:2, :]], axis=1)
    diag_g = (grecv[0] + grecv[1])[0:1, :] * (1.0 / tokens)
    diag_g = jnp.broadcast_to(diag_g, (rows, rows)).T
    diag_g = jnp.concatenate([diag_g] * (block // rows), axis=1)
    scaled = (rotated / (diag_g * diag_a + damping)).astype(jnp.bfloat16)
    back = dot(qa[...], scaled, 1, 1).astype(jnp.bfloat16)
    bsend[...] = back.reshape(bsend.shape)
    send_all(back_copy, bsend, brecv)

    @pl.loop(1, places)
    def _(step):
        factor_copy(step).wait_recv()

    total = fsend[place].astype(jnp.float32)
    for step in range(1, places):
        total = total + frecv[step].astype(jnp.float32)
    fsum[...] = total
    away_a = fsum[pl.ds(pl.multiple_of((1 - zh) * rows_a, 8), rows_a), :]
    away_g = fsum[pl.ds(pl.multiple_of(2 * rows_a + (1 - zh) * rows_g, 8), rows_g), :]
    fzsend[0:2 * rows_a, :] = jnp.concatenate([away_a[:, :half], away_a[:, half:]], axis=0).astype(jnp.bfloat16)
    fzsend[2 * rows_a:, :] = jnp.concatenate([away_g[:, :half], away_g[:, half:]], axis=0).astype(jnp.bfloat16)
    fz_copy = pltpu.make_async_remote_copy(
        src_ref=fzsend, dst_ref=fzrecv, send_sem=fz_sem.at[0], recv_sem=fz_sem.at[1],
        device_id=across, device_id_type=MESH,
    )
    fz_copy.start()

    receive_all(back_copy)
    for b in range(pg.shape[0] // block):
        lot = jnp.concatenate([brecv[b * per_block + i] for i in range(per_block)], axis=1)
        op[:, b * block:(b + 1) * block] = dot(lot, pg[b * block:(b + 1) * block, :], 1, 1)
    out_p = pltpu.make_async_copy(op, op_out, out_sem.at[0])
    out_p.start()

    fz_copy.wait_recv()
    here_a = fsum[pl.ds(pl.multiple_of(zh * rows_a, 8), rows_a), :]
    here_g = fsum[pl.ds(pl.multiple_of(2 * rows_a + zh * rows_g, 8), rows_g), :]
    there = fzrecv[...].astype(jnp.float32)
    there_a = jnp.concatenate([there[:rows_a], there[rows_a:2 * rows_a]], axis=1)
    there_g = jnp.concatenate([there[2 * rows_a:2 * rows_a + rows_g], there[2 * rows_a + rows_g:]], axis=1)
    oa[...] = (here_a + there_a) * (1.0 / tokens)
    og[...] = (here_g + there_g) * (1.0 / tokens)
    out_a = pltpu.make_async_copy(oa, oa_out, out_sem.at[1])
    out_g = pltpu.make_async_copy(og, og_out, out_sem.at[2])
    out_a.start()
    out_g.start()

    swap_a.wait_send()
    swap_g.wait_send()
    drain_all(left_copy)
    drain_all(back_copy)

    @pl.loop(1, places)
    def _(step):
        diag_copy(step).wait_send()
        factor_copy(step).wait_send()

    dz_copy.wait_send()
    g_copy(other, 1).wait_send()

    @pl.when(jnp.logical_not(diagonal))
    def _():
        g_copy(lane, 0).wait_send()

    fz_copy.wait_send()
    out_p.wait()
    out_a.wait()
    out_g.wait()


def shards(ny, nx, activations, out_grads, grad_weight, basis_a, basis_g):
    replicas = lax.axis_size("dp")
    here, block = activations.shape
    tokens = here * replicas
    wide = out_grads.shape[1]
    rows, cols = grad_weight.shape
    rows_a, rows_g = block // replicas, wide // replicas
    places = ny * nx
    chunk = rows // CHUNKS
    bf16, f32 = jnp.bfloat16, jnp.float32
    dma = pltpu.SemaphoreType.DMA
    vmem = pltpu.VMEM
    scratch = [
        vmem((2, here, block), bf16), vmem((2, here, wide), bf16), vmem((cols, rows), bf16),
        vmem((block, block), bf16), vmem((wide, block), bf16),
        vmem((CHUNKS, cols, chunk), bf16), vmem((CHUNKS, cols, chunk), bf16),
        vmem((CHUNKS, cols, chunk), bf16), vmem((CHUNKS, cols, chunk), bf16),
        vmem((8, block // 2), f32), vmem((places, 8, block // 2), f32),
        vmem((8, block // 2), f32), vmem((8, block // 2), f32),
        vmem((CHUNKS, 8, 128), f32), vmem((2, 8, 128), f32),
        vmem((places, 2 * rows_a + 2 * rows_g, block), bf16),
        vmem((places, 2 * rows_a + 2 * rows_g, block), bf16),
        vmem((2 * rows_a + 2 * rows_g, block), f32),
        vmem((2 * rows_a + 2 * rows_g, block // 2), bf16),
        vmem((2 * rows_a + 2 * rows_g, block // 2), bf16),
        vmem((rows_a, block), f32), vmem((rows_g, block), f32), vmem((cols, rows), f32),
        dma((5,)), dma((2,)), dma((2,)),
        dma((CHUNKS,)), dma((CHUNKS,)), dma((CHUNKS,)), dma((CHUNKS,)),
        dma((places,)), dma((places,)), dma((2,)), dma((2,)), dma((2,)),
        dma((places,)), dma((places,)), dma((2,)), dma((3,)),
    ]
    anywhere = pl.BlockSpec(memory_space=pl.ANY)
    factor_a, factor_g, precond = pl.pallas_call(
        functools.partial(kernel, ny, nx, tokens),
        out_shape=(
            jax.ShapeDtypeStruct((rows_a, block), f32),
            jax.ShapeDtypeStruct((rows_g, block), f32),
            jax.ShapeDtypeStruct((cols, rows), f32),
        ),
        in_specs=[anywhere] * 5,
        out_specs=(anywhere,) * 3,
        scratch_shapes=scratch,
        compiler_params=pltpu.CompilerParams(
            collective_id=0, has_side_effects=True, vmem_limit_bytes=40 * 1024 * 1024
        ),
    )(activations, out_grads, grad_weight.T, basis_a, basis_g)
    return factor_a, factor_g, precond.T


def solution(mesh):
    side = {64: 4, 16: 2}[mesh.shape["dp"]]
    in_specs = (P("dp", "mp"), P("dp", "mp"), P("mp", "dp"), P("mp", None), P("mp", None))
    out_specs = (P(("mp", "dp"), None), P(("mp", "dp"), None), P("mp", "dp"))
    return jax.shard_map(
        functools.partial(shards, side, side), mesh=mesh, in_specs=in_specs, out_specs=out_specs, check_vma=False
    )
```

time: 1250 us -> 71.5 us (0.06)
  the two profiles are of different devices: /device:TPU:1 before, /device:TPU:24 now
where the time goes in v1:
time: 71.5 us; the launch traced here: 71.2 us
  Pallas kernels  63.7 us (89%)
  local copies, waits for them, and re-layouts  6.94 us (10%)
    pallas_call x1, Pallas kernels, shards(): pl.pallas_call(functools.partial(kernel, ny, nx, tokens), out_shape=(jax....  63.7 us
    unnamed x13, local copies, waits for them, and re-layouts  6.94 us

profile of v1, /device:TPU:24, one launch (start us, length us, event | category | flops | bytes accessed | tf_op | source)
XLA Modules:
  0.0 71.2 jit_solution(17677481476920743116)
XLA Ops:
  0.6 0.0 copy-start
  0.6 1.2 %copy-done = bf16[1024,512]{1,0:T(8,128)(2,1)S(1)} copy-done((bf16[1024,512]{1,0:T(8,128)(2,1)S(1)}, bf16[1024,512]{1,0:T(8,128)(2,1)}, u32[]{:S(2)}) %copy-start) | copy-done | bytes 1048600
  1.9 0.0 copy-start.1
  1.9 1.0 %copy-done.1 = bf16[512,512]{1,0:T(8,128)(2,1)S(1)} copy-done((bf16[512,512]{1,0:T(8,128)(2,1)S(1)}, bf16[512,512]{1,0:T(8,128)(2,1)}, u32[]{:S(2)}) %copy-start.1) | copy-done | bytes 524312
  2.9 0.0 copy-start.2
  2.9 0.9 %copy-done.2 = bf16[128,1024]{1,0:T(8,128)(2,1)S(1)} copy-done((bf16[128,1024]{1,0:T(8,128)(2,1)S(1)}, bf16[128,1024]{1,0:T(8,128)(2,1)}, u32[]{:S(2)}) %copy-start.2) | copy-done | bytes 262168
  3.9 0.0 copy-start.3
  3.9 0.9 %copy-done.3 = bf16[128,512]{1,0:T(8,128)(2,1)S(1)} copy-done((bf16[128,512]{1,0:T(8,128)(2,1)S(1)}, bf16[128,512]{1,0:T(8,128)(2,1)}, u32[]{:S(2)}) %copy-start.3) | copy-done | bytes 131096
  4.8 0.0 copy-start.4
  4.8 0.9 %copy-done.4 = bf16[1024,64]{0,1:T(8,128)(2,1)S(1)} copy-done((bf16[1024,64]{0,1:T(8,128)(2,1)S(1)}, bf16[1024,64]{0,1:T(8,128)(2,1)}, u32[]{:S(2)}) %copy-start.4) | copy-done | bytes 131096
  5.7 63.7 %shard_map.76 = (f32[8,512]{1,0:T(8,128)S(1)}, f32[16,512]{1,0:T(8,128)S(1)}, f32[64,1024]{1,0:T(8,128)S(1)}) custom-call(bf16[128,512]{1,0:T(8,128)(2,1)S(1)} %copy-done.3, bf16[128,1024]{1,0:T(8,128)(2,1)S(1)} %copy-done.2, bf16[64,1024]{1,0:T(8,128)(2,1)S(1)} %bitcast.3, bf16[512,512]{1,0:T(8,128)(2,1)S(1)} %copy-done.1, bf16[1024,512]{1,0:T(8,128)(2,1)S(1)} %copy-done), custom_call_target="tpu_custom_call" | custom-call | tf_op jit(solution)/shard_map/pallas_call | solution.py:365
  69.3 0.6 copy.11
  69.9 0.6 copy.12
  70.5 0.7 copy.13
Async XLA Ops:
  0.6 1.2 %copy-start = (bf16[1024,512]{1,0:T(8,128)(2,1)S(1)}, bf16[1024,512]{1,0:T(8,128)(2,1)}, u32[]{:S(2)}) copy-start(bf16[1024,512]{1,0:T(8,128)(2,1)} %pg_in.1) | copy-start | bytes 3145732
  1.9 1.0 %copy-start.1 = (bf16[512,512]{1,0:T(8,128)(2,1)S(1)}, bf16[512,512]{1,0:T(8,128)(2,1)}, u32[]{:S(2)}) copy-start(bf16[512,512]{1,0:T(8,128)(2,1)} %qa_in.1) | copy-start | bytes 1572868
  2.9 0.9 %copy-start.2 = (bf16[128,1024]{1,0:T(8,128)(2,1)S(1)}, bf16[128,1024]{1,0:T(8,128)(2,1)}, u32[]{:S(2)}) copy-start(bf16[128,1024]{1,0:T(8,128)(2,1)} %xg_in.1) | copy-start | bytes 786436
  3.9 0.9 %copy-start.3 = (bf16[128,512]{1,0:T(8,128)(2,1)S(1)}, bf16[128,512]{1,0:T(8,128)(2,1)}, u32[]{:S(2)}) copy-start(bf16[128,512]{1,0:T(8,128)(2,1)} %xa_in.1) | copy-start | bytes 393220
  4.8 0.9 %copy-start.4 = (bf16[1024,64]{0,1:T(8,128)(2,1)S(1)}, bf16[1024,64]{0,1:T(8,128)(2,1)}, u32[]{:S(2)}) copy-start(bf16[1024,64]{0,1:T(8,128)(2,1)} %param.7) | copy-start | bytes 393220

commit v2 on v1

v2 whole, which is shorter than its diff:
```python
import functools

import jax
import jax.numpy as jnp
from jax import lax
from jax.experimental import pallas as pl
from jax.experimental.pallas import tpu as pltpu
from jax.sharding import PartitionSpec as P

MESH = pl.DeviceIdType.MESH
damping = 0.01
CHUNKS = 8


def dot(a, b, dim_a, dim_b):
    return lax.dot_general(a, b, (((dim_a,), (dim_b,)), ((), ())), preferred_element_type=jnp.float32)


def row_picker(size, group, core):
    row = lax.broadcasted_iota(jnp.int32, (size, size // 2), 0)
    col = lax.broadcasted_iota(jnp.int32, (size, size // 2), 1)
    within = lax.rem(col, group)
    return jnp.where(row == (col - within) * 2 + group * core + within, 1.0, 0.0).astype(jnp.bfloat16)


def kernel(
    ny, nx, levels, tokens,
    xa_in, xg_in, w_in, qa_in, pg_in,
    oa_out, og_out, op_out,
    xa, xg, w, qa, pg, qj,
    lsend, lrecv, bsend, brecv,
    dsend, drecv, dtwin, dsum, grecv, arecv,
    fsend, frecv, fzsend, fzrecv,
    oa, og, op,
    load_sem, core_send, core_recv, q_send, q_recv, twin_sem,
    lsend_sem, lrecv_sem, bsend_sem, brecv_sem,
    dsend_sem, drecv_sem, gsend_sem, grecv_sem, asend_sem, arecv_sem, dtwin_sem, answer_across, answer_column,
    fsend_sem, frecv_sem, fz_sem, out_sem,
):
    d = lax.axis_index("dp")
    m = lax.axis_index("mp")
    core = lax.rem(d, 2)
    zh = lax.rem(d // 2, 2)
    place = d // 4
    x = lax.rem(place, nx)
    y = place // nx
    places = ny * nx
    group = d // CHUNKS
    lane = lax.rem(d, CHUNKS)
    z = zh * levels + m
    source = group == m
    reach = levels // 2
    spread = nx // 2
    gives = lax.rem(m, spread) == x // 2
    given_y = m // spread
    odd = lax.rem(y, 2)
    late = zh == 1
    facing = lax.rem(m + reach, levels)
    rows_a, rows_g = oa.shape[0], og.shape[0]
    block = qa.shape[0]
    cols = w.shape[0]

    twin = (d + 1 - 2 * core, m)
    across = (d + 2 - 4 * zh, m)

    def peer(step, sign):
        dy, dx = step // nx, lax.rem(step, nx)
        to_y = lax.rem(y + sign * dy + ny, ny)
        to_x = lax.rem(x + sign * dx + nx, nx)
        return to_y * nx + to_x

    def at_place(p):
        return (p * 4 + zh * 2 + core, m)

    def friend(q):
        return (group * CHUNKS + q, facing)

    def at_height(to):
        to = lax.rem(to + 2 * levels, 2 * levels)
        return (place * 4 + (to // levels) * 2 + core, lax.rem(to, levels))

    loads = [
        pltpu.make_async_copy(src, dst, load_sem.at[i])
        for i, (src, dst) in enumerate(
            ((w_in, w), (pg_in, pg), (xa_in, xa.at[0]), (xg_in, xg.at[0]), (qa_in, qa))
        )
    ]
    for load in loads:
        load.start()

    barrier = pltpu.get_barrier_semaphore()

    def greet(device):
        pl.semaphore_signal(barrier, inc=1, device_id=device, device_id_type=MESH)

    greet(twin)

    @pl.loop(1, places)
    def _(step):
        greet(at_place(peer(step, 1)))

    @pl.loop(0, CHUNKS)
    def _(q):
        greet(friend(q))

    def at_yz(to_y, to):
        to = lax.rem(to + 2 * levels, 2 * levels)
        return ((to_y * nx + x) * 4 + (to // levels) * 2 + core, lax.rem(to, levels))

    above = lax.rem(m - group + levels, levels)

    def giver_level(from_y):
        up = jnp.logical_or(above < reach, jnp.logical_and(above == reach, lax.rem(from_y, 2) == 0))
        return jnp.where(up, z - above, z - above + levels)

    for from_y in range(ny):
        @pl.when(jnp.logical_not(jnp.logical_and(source, y == from_y)))
        def _():
            greet(at_yz(from_y, giver_level(from_y)))

    @pl.when(jnp.logical_not(source))
    def _():
        greet(at_height(group + zh * levels))

    @pl.when(jnp.logical_not(late))
    def _():
        greet(across)
        greet(at_height(group + levels))

        @pl.when(source)
        def _():
            @pl.loop(0, levels)
            def _(to):
                greet(at_height(levels + to))

    count = 1 + places - 1 + CHUNKS
    count += jnp.where(gives, levels, 0) - jnp.where(source, 1, 0)
    count += jnp.where(source, levels - 1, 0)
    count += jnp.where(late, 2, 0) + jnp.where(jnp.logical_and(source, late), levels, 0)

    loads[0].wait()
    loads[1].wait()
    per_block = block // lsend.shape[2]
    for b in range(pg.shape[0] // block):
        left = dot(w[:, b * block:(b + 1) * block], pg[b * block:(b + 1) * block, :], 1, 0)
        left = left.astype(jnp.bfloat16)
        for i in range(per_block):
            lsend[b * per_block + i] = left[:, i * lsend.shape[2]:(i + 1) * lsend.shape[2]]

    for load in loads[2:]:
        load.wait()
    sides = [(xa[0], qa[...])] + [
        (xg[0, :, b * block:(b + 1) * block], pg[b * block:(b + 1) * block, :])
        for b in range(pg.shape[0] // block)
    ]
    totals = []
    for values, basis in sides:
        turned = dot(values, basis, 1, 0)
        totals.append(jnp.sum(turned * turned, axis=0, keepdims=True))
    strips = [total[:, i * 128:(i + 1) * 128] for total in totals for i in range(block // 128)]
    strips_a, strips_g = strips[:4], strips[4:]
    for side in range(2):
        dsend[side] = jnp.concatenate(strips_g[side * 4:side * 4 + 4] + strips_a, axis=0)

    pl.semaphore_wait(barrier, count)

    @pl.when(late)
    def _():
        pl.semaphore_signal(answer_across, inc=1, device_id=across, device_id_type=MESH)
        pl.semaphore_signal(answer_column, inc=1, device_id=at_height(group), device_id_type=MESH)

    def diag_copy(step):
        to = peer(step, 1)
        return pltpu.make_async_remote_copy(
            src_ref=dsend.at[lax.rem(to, 2)], dst_ref=drecv.at[step],
            send_sem=dsend_sem.at[step], recv_sem=drecv_sem.at[step],
            device_id=at_place(to), device_id_type=MESH,
        )

    @pl.loop(1, places)
    def _(step):
        diag_copy(step).start()

    swap_a = pltpu.make_async_remote_copy(
        src_ref=xa_in, dst_ref=xa.at[1], send_sem=core_send.at[0], recv_sem=core_recv.at[0],
        device_id=twin, device_id_type=MESH,
    )
    swap_g = pltpu.make_async_remote_copy(
        src_ref=xg_in, dst_ref=xg.at[1], send_sem=core_send.at[1], recv_sem=core_recv.at[1],
        device_id=twin, device_id_type=MESH,
    )
    swap_a.start()
    swap_g.start()

    part = block // ny // 2

    def q_copy(step, from_y):
        return pltpu.make_async_remote_copy(
            src_ref=qa.at[pl.ds(pl.multiple_of((y * 2 + core) * part, 16), part)],
            dst_ref=qj.at[from_y, core],
            send_sem=q_send.at[step], recv_sem=q_recv.at[from_y],
            device_id=at_yz(given_y, z + step + 1 - odd - reach), device_id_type=MESH,
        )

    def q_is_own(step):
        return jnp.logical_and(source, step + 1 - odd == reach)

    @pl.when(gives)
    def _():
        @pl.loop(0, levels)
        def _(step):
            @pl.when(jnp.logical_not(q_is_own(step)))
            def _():
                q_copy(step, y).start()

    to_twin = pltpu.make_async_remote_copy(
        src_ref=qj.at[:, core], dst_ref=qj.at[:, core],
        send_sem=twin_sem.at[0], recv_sem=twin_sem.at[1],
        device_id=twin, device_id_type=MESH,
    )

    def left_copy(q, slot):
        return pltpu.make_async_remote_copy(
            src_ref=lsend.at[q], dst_ref=lrecv.at[slot],
            send_sem=lsend_sem.at[q], recv_sem=lrecv_sem.at[slot],
            device_id=friend(q), device_id_type=MESH,
        )

    def back_copy(q, slot):
        return pltpu.make_async_remote_copy(
            src_ref=bsend.at[q], dst_ref=brecv.at[slot],
            send_sem=bsend_sem.at[q], recv_sem=brecv_sem.at[slot],
            device_id=friend(q), device_id_type=MESH,
        )

    def send_all(copy):
        @pl.loop(0, CHUNKS)
        def _(q):
            copy(q, lane).start()

    def receive_all(copy):
        @pl.loop(0, CHUNKS)
        def _(k):
            copy(k, k).wait_recv()

    def drain_all(copy):
        @pl.loop(0, CHUNKS)
        def _(q):
            copy(q, lane).wait_send()

    send_all(left_copy)

    swap_a.wait_recv()
    swap_g.wait_recv()
    xa_all = xa[...].reshape(-1, block)
    xg_all = [
        xg[:, :, b * block:(b + 1) * block].reshape(-1, block) for b in range(pg.shape[0] // block)
    ]
    half = block // 2

    pick_a = row_picker(block, rows_a, core)
    pick_g = row_picker(block, rows_g, core)
    picked = dot(xa_all, pick_a, 1, 0).astype(jnp.bfloat16)
    product = dot(picked, xa_all, 0, 0).reshape(places, 2, rows_a, block)
    product = jnp.concatenate([product[..., :half], product[..., half:]], axis=2).astype(jnp.bfloat16)
    for side in range(2):
        fsend[side, :, :, 0:half] = product[:, side]
    each = places // len(xg_all)
    for b, values in enumerate(xg_all):
        picked = dot(values, pick_g, 1, 0).astype(jnp.bfloat16)
        product = dot(picked, values, 0, 0).astype(jnp.bfloat16).reshape(each, 2, rows_g, block)
        for side in range(2):
            fsend[side, b * each:(b + 1) * each, :, half:] = product[:, side]

    def factor_copy(side, step):
        to = peer(step, 1)
        return pltpu.make_async_remote_copy(
            src_ref=fsend.at[side, to], dst_ref=frecv.at[side, step],
            send_sem=fsend_sem.at[side, step], recv_sem=frecv_sem.at[side, step],
            device_id=at_place(to), device_id_type=MESH,
        )

    for side in (1 - zh, zh):
        @pl.loop(1, places)
        def _(step):
            factor_copy(side, step).start()

    drecv[0] = dsend[lax.rem(x, 2)]

    @pl.loop(1, places)
    def _(step):
        diag_copy(step).wait_recv()

    dtwin[0] = jnp.sum(drecv[...], axis=0)
    d_copy = pltpu.make_async_remote_copy(
        src_ref=dtwin.at[0], dst_ref=dtwin.at[1], send_sem=dtwin_sem.at[0], recv_sem=dtwin_sem.at[1],
        device_id=twin, device_id_type=MESH,
    )
    d_copy.start()
    d_copy.wait_recv()
    dsum[...] = dtwin[0] + dtwin[1]

    def g_copy(side, slot):
        return pltpu.make_async_remote_copy(
            src_ref=dsum, dst_ref=grecv.at[slot],
            send_sem=gsend_sem.at[side], recv_sem=grecv_sem.at[slot],
            device_id=(place * 4 + side * 2 + core, facing), device_id_type=MESH,
        )

    for side in range(2):
        g_copy(side, zh).start()

    def a_copy(step, slot):
        return pltpu.make_async_remote_copy(
            src_ref=dsum, dst_ref=arecv.at[slot],
            send_sem=asend_sem.at[step], recv_sem=arecv_sem.at[slot],
            device_id=at_height(z + step), device_id_type=MESH,
        )

    @pl.when(source)
    def _():
        @pl.when(jnp.logical_not(late))
        def _():
            pl.semaphore_wait(answer_column, levels)

        @pl.loop(1, 2 * levels)
        def _(step):
            a_copy(step, zh).start()

        arecv[pl.ds(zh, 1)] = dsum[...].reshape(1, 8, 128)

    @pl.when(source)
    def _():
        qj[y, core] = qa[pl.ds(pl.multiple_of((y * 2 + core) * part, 16), part), :]

    for from_y in range(ny):
        @pl.when(jnp.logical_not(jnp.logical_and(source, y == from_y)))
        def _():
            q_copy(0, from_y).wait_recv()

    to_twin.start()

    receive_all(left_copy)
    rows = lrecv.shape[2]
    to_twin.wait_recv()
    rotated = dot(lrecv[...].reshape(block, rows), qj[...].reshape(block, block), 0, 0)

    @pl.when(source)
    def _():
        a_copy(1, 1 - zh).wait_recv()

    @pl.when(jnp.logical_not(source))
    def _():
        for slot in range(2):
            a_copy(1, slot).wait_recv()

    for slot in range(2):
        g_copy(0, slot).wait_recv()

    both_a = (arecv[0] + arecv[1]) * (1.0 / tokens)
    diag_a = jnp.concatenate([both_a[4 + i:5 + i, :] for i in range(block // 128)], axis=1)
    both_g = (grecv[0] + grecv[1]) * (1.0 / tokens)
    first = jnp.where(core == 0, both_g[0:1, :], both_g[1:2, :])
    second = jnp.where(core == 0, both_g[2:3, :], both_g[3:4, :])
    diag_g = jnp.where(zh == 0, first, second)
    diag_g = jnp.broadcast_to(diag_g, (rows, rows)).T
    diag_g = jnp.concatenate([diag_g] * (block // rows), axis=1)
    scaled = (rotated / (diag_g * diag_a + damping)).astype(jnp.bfloat16)
    back = dot(qj[...].reshape(block, block), scaled, 1, 1).astype(jnp.bfloat16)
    bsend[...] = back.reshape(bsend.shape)
    send_all(back_copy)

    def plane_sum(side):
        @pl.loop(1, places)
        def _(step):
            factor_copy(side, step).wait_recv()

        total = fsend[side, place].astype(jnp.float32)
        for step in range(1, places):
            total = total + frecv[side, step].astype(jnp.float32)
        return total

    fzsend[...] = plane_sum(1 - zh).astype(jnp.bfloat16)
    fz_copy = pltpu.make_async_remote_copy(
        src_ref=fzsend, dst_ref=fzrecv, send_sem=fz_sem.at[0], recv_sem=fz_sem.at[1],
        device_id=across, device_id_type=MESH,
    )

    @pl.when(jnp.logical_not(late))
    def _():
        pl.semaphore_wait(answer_across, 1)

    fz_copy.start()
    here = plane_sum(zh)

    receive_all(back_copy)
    for b in range(pg.shape[0] // block):
        lot = jnp.concatenate([brecv[b * per_block + i] for i in range(per_block)], axis=1)
        op[:, b * block:(b + 1) * block] = dot(lot, pg[b * block:(b + 1) * block, :], 1, 1)
    out_p = pltpu.make_async_copy(op, op_out, out_sem.at[0])
    out_p.start()

    fz_copy.wait_recv()
    both = (here + fzrecv[...].astype(jnp.float32)) * (1.0 / tokens)
    oa[...] = jnp.concatenate([both[:rows_a, :half], both[rows_a:, :half]], axis=1)
    og[...] = both[:, half:]
    out_a = pltpu.make_async_copy(oa, oa_out, out_sem.at[1])
    out_g = pltpu.make_async_copy(og, og_out, out_sem.at[2])
    out_a.start()
    out_g.start()

    swap_a.wait_send()
    swap_g.wait_send()
    drain_all(left_copy)
    drain_all(back_copy)

    @pl.loop(1, places)
    def _(step):
        diag_copy(step).wait_send()
        factor_copy(0, step).wait_send()
        factor_copy(1, step).wait_send()

    for side in range(2):
        g_copy(side, zh).wait_send()

    @pl.when(source)
    def _():
        @pl.loop(1, 2 * levels)
        def _(step):
            a_copy(step, zh).wait_send()

    @pl.when(gives)
    def _():
        @pl.loop(0, levels)
        def _(step):
            @pl.when(jnp.logical_not(q_is_own(step)))
            def _():
                q_copy(step, y).wait_send()

    to_twin.wait_send()
    d_copy.wait_send()
    fz_copy.wait_send()
    out_p.wait()
    out_a.wait()
    out_g.wait()


def shards(ny, nx, activations, out_grads, grad_weight, basis_a, basis_g):
    replicas = lax.axis_size("dp")
    here, block = activations.shape
    tokens = here * replicas
    wide = out_grads.shape[1]
    rows, cols = grad_weight.shape
    rows_a, rows_g = block // replicas, wide // replicas
    places = ny * nx
    levels = lax.axis_size("mp")
    chunk = rows // CHUNKS
    bf16, f32 = jnp.bfloat16, jnp.float32
    dma = pltpu.SemaphoreType.DMA
    vmem = pltpu.VMEM
    scratch = [
        vmem((2, here, block), bf16), vmem((2, here, wide), bf16), vmem((cols, rows), bf16),
        vmem((block, block), bf16), vmem((wide, block), bf16), vmem((ny, 2, block // ny // 2, block), bf16),
        vmem((CHUNKS, cols, chunk), bf16), vmem((CHUNKS, cols, chunk), bf16),
        vmem((CHUNKS, cols, chunk), bf16), vmem((CHUNKS, cols, chunk), bf16),
        vmem((2, 8, 128), f32), vmem((places, 8, 128), f32), vmem((2, 8, 128), f32), vmem((8, 128), f32),
        vmem((2, 8, 128), f32), vmem((2, 8, 128), f32),
        vmem((2, places, rows_g, block + block // 2), bf16),
        vmem((2, places, rows_g, block + block // 2), bf16),
        vmem((rows_g, block + block // 2), bf16),
        vmem((rows_g, block + block // 2), bf16),
        vmem((rows_a, block), f32), vmem((rows_g, block), f32), vmem((cols, rows), f32),
        dma((5,)), dma((2,)), dma((2,)), dma((levels,)), dma((ny,)), dma((2,)),
        dma((CHUNKS,)), dma((CHUNKS,)), dma((CHUNKS,)), dma((CHUNKS,)),
        dma((places,)), dma((places,)), dma((2,)), dma((2,)), dma((2 * levels,)), dma((2,)), dma((2,)),
        pltpu.SemaphoreType.REGULAR, pltpu.SemaphoreType.REGULAR,
        dma((2, places)), dma((2, places)), dma((2,)), dma((3,)),
    ]
    anywhere = pl.BlockSpec(memory_space=pltpu.HBM)
    factor_a, factor_g, precond = pl.pallas_call(
        functools.partial(kernel, ny, nx, levels, tokens),
        out_shape=(
            jax.ShapeDtypeStruct((rows_a, block), f32),
            jax.ShapeDtypeStruct((rows_g, block), f32),
            jax.ShapeDtypeStruct((cols, rows), f32),
        ),
        in_specs=[anywhere] * 5,
        out_specs=(anywhere,) * 3,
        scratch_shapes=scratch,
        compiler_params=pltpu.CompilerParams(
            collective_id=0, has_side_effects=True, vmem_limit_bytes=60 * 1024 * 1024
        ),
    )(activations, out_grads, grad_weight.T, basis_a, basis_g)
    return factor_a, factor_g, precond.T


def solution(mesh):
    side = {64: 4, 16: 2}[mesh.shape["dp"]]
    in_specs = (P("dp", "mp"), P("dp", "mp"), P("mp", "dp"), P("mp", None), P("mp", None))
    out_specs = (P(("mp", "dp"), None), P(("mp", "dp"), None), P("mp", "dp"))
    return jax.shard_map(
        functools.partial(shards, side, side), mesh=mesh, in_specs=in_specs, out_specs=out_specs, check_vma=False
    )
```

time: 71.5 us -> 53.2 us (0.74)
  the two profiles are of different devices: /device:TPU:24 before, /device:TPU:5 now
where the time goes in v2:
time: 53.2 us; the launch traced here: 52.9 us
  Pallas kernels  48.7 us (92%)
  local copies, waits for them, and re-layouts  3.62 us (7%)
  between operations  0.65 us (1%)
    pallas_call x1, Pallas kernels, shards(): pl.pallas_call(functools.partial(kernel, ny, nx, levels, tokens), out_sha...  48.7 us
    unnamed x5, local copies, waits for them, and re-layouts  3.62 us

profile of v2, /device:TPU:5, one launch (start us, length us, event | category | flops | bytes accessed | tf_op | source)
XLA Modules:
  0.0 52.9 jit_solution(6448559187748593893)
XLA Ops:
  0.6 48.7 %shard_map.76 = (f32[8,512]{1,0:T(8,128)}, f32[16,512]{1,0:T(8,128)}, f32[64,1024]{1,0:T(8,128)}) custom-call(bf16[128,512]{1,0:T(8,128)(2,1)} %xa_in.1, bf16[128,1024]{1,0:T(8,128)(2,1)} %xg_in.1, bf16[64,1024]{1,0:T(8,128)(2,1)} %bitcast.3, bf16[512,512]{1,0:T(8,128)(2,1)} %qa_in.1, bf16[1024,512]{1,0:T(8,128)(2,1)} %pg_in.1), custom_call_target="tpu_custom_call" | custom-call | tf_op jit(solution)/shard_map/pallas_call | solution.py:480
  49.3 0.0 copy-start
  49.3 1.3 %copy.11 = f32[8,512]{1,0:T(8,128)} copy(f32[8,512]{1,0:T(8,128)} %get-tuple-element.12) | data formatting | bytes 32768
  50.6 0.0 copy-done
  50.7 0.6 %copy.12 = f32[16,512]{1,0:T(8,128)} copy(f32[16,512]{1,0:T(8,128)S(1)} %copy-done) | data formatting | bytes 65536
  51.3 1.7 %copy.13 = f32[1024,64]{0,1:T(8,128)} copy(f32[1024,64]{0,1:T(8,128)} %bitcast.2) | data formatting | bytes 524288
Async XLA Ops:
  49.3 1.3 %copy-start = (f32[16,512]{1,0:T(8,128)S(1)}, f32[16,512]{1,0:T(8,128)}, u32[]{:S(2)}) copy-start(f32[16,512]{1,0:T(8,128)} %get-tuple-element.13) | copy-start | bytes 98308

commit v3 on v2

--- a/solution.py
+++ b/solution.py
@@ -24,14 +24,13 @@
 
 
 def kernel(
-    ny, nx, levels, tokens,
+    ny, nx, levels, tokens, rows_a, rows_g,
     xa_in, xg_in, w_in, qa_in, pg_in,
-    oa_out, og_out, op_out,
+    here_out, fzrecv, brecv,
     xa, xg, w, qa, pg, qj,
-    lsend, lrecv, bsend, brecv,
+    lsend, lrecv, bsend,
     dsend, drecv, dtwin, dsum, grecv, arecv,
-    fsend, frecv, fzsend, fzrecv,
-    oa, og, op,
+    fsend, frecv, fzsend, here,
     load_sem, core_send, core_recv, q_send, q_recv, twin_sem,
     lsend_sem, lrecv_sem, bsend_sem, brecv_sem,
     dsend_sem, drecv_sem, gsend_sem, grecv_sem, asend_sem, arecv_sem, dtwin_sem, answer_across, answer_column,
@@ -53,10 +52,9 @@
     spread = nx // 2
     gives = lax.rem(m, spread) == x // 2
     given_y = m // spread
-    odd = lax.rem(y, 2)
+    odd = core
     late = zh == 1
     facing = lax.rem(m + reach, levels)
-    rows_a, rows_g = oa.shape[0], og.shape[0]
     block = qa.shape[0]
     cols = w.shape[0]
 
@@ -85,38 +83,11 @@
             ((w_in, w), (pg_in, pg), (xa_in, xa.at[0]), (xg_in, xg.at[0]), (qa_in, qa))
         )
     ]
-    for load in loads:
-        load.start()
 
     barrier = pltpu.get_barrier_semaphore()
 
     def greet(device):
         pl.semaphore_signal(barrier, inc=1, device_id=device, device_id_type=MESH)
-
-    greet(twin)
-
-    @pl.loop(1, places)
-    def _(step):
-        greet(at_place(peer(step, 1)))
-
-    @pl.loop(0, CHUNKS)
-    def _(q):
-        greet(friend(q))
-
-    def at_yz(to_y, to):
-        to = lax.rem(to + 2 * levels, 2 * levels)
-        return ((to_y * nx + x) * 4 + (to // levels) * 2 + core, lax.rem(to, levels))
-
-    above = lax.rem(m - group + levels, levels)
-
-    def giver_level(from_y):
-        up = jnp.logical_or(above < reach, jnp.logical_and(above == reach, lax.rem(from_y, 2) == 0))
-        return jnp.where(up, z - above, z - above + levels)
-
-    for from_y in range(ny):
-        @pl.when(jnp.logical_not(jnp.logical_and(source, y == from_y)))
-        def _():
-            greet(at_yz(from_y, giver_level(from_y)))
 
     @pl.when(jnp.logical_not(source))
     def _():
@@ -132,6 +103,34 @@
             @pl.loop(0, levels)
             def _(to):
                 greet(at_height(levels + to))
+
+    def at_yz(to_y, to):
+        to = lax.rem(to + 2 * levels, 2 * levels)
+        return ((to_y * nx + x) * 4 + (to // levels) * 2 + core, lax.rem(to, levels))
+
+    above = lax.rem(m - group + levels, levels)
+
+    def giver_level(from_y):
+        up = jnp.logical_or(above < reach, jnp.logical_and(above == reach, core == 0))
+        return jnp.where(up, z - above, z - above + levels)
+
+    for from_y in range(ny):
+        @pl.when(jnp.logical_not(jnp.logical_and(source, y == from_y)))
+        def _():
+            greet(at_yz(from_y, giver_level(from_y)))
+
+    greet(twin)
+
+    @pl.loop(1, places)
+    def _(step):
+        greet(at_place(peer(step, 1)))
+
+    @pl.loop(0, CHUNKS)
+    def _(q):
+        greet(friend(q))
+
+    for load in loads:
+        load.start()
 
     count = 1 + places - 1 + CHUNKS
     count += jnp.where(gives, levels, 0) - jnp.where(source, 1, 0)
@@ -167,7 +166,7 @@
     @pl.when(late)
     def _():
         pl.semaphore_signal(answer_across, inc=1, device_id=across, device_id_type=MESH)
-        pl.semaphore_signal(answer_column, inc=1, device_id=at_height(group), device_id_type=MESH)
+        pl.semaphore_signal(answer_column.at[m], inc=1, device_id=at_height(group), device_id_type=MESH)
 
     def diag_copy(step):
         to = peer(step, 1)
@@ -248,7 +247,6 @@
         def _(q):
             copy(q, lane).wait_send()
 
-    send_all(left_copy)
 
     swap_a.wait_recv()
     swap_g.wait_recv()
@@ -285,6 +283,8 @@
         def _(step):
             factor_copy(side, step).start()
 
+    send_all(left_copy)
+
     drecv[0] = dsend[lax.rem(x, 2)]
 
     @pl.loop(1, places)
@@ -317,17 +317,57 @@
             device_id=at_height(z + step), device_id_type=MESH,
         )
 
+    @pl.when(jnp.logical_and(source, late))
+    def _():
+        @pl.loop(1, 2 * levels)
+        def _(step):
+            a_copy(step, zh).start()
+
+    @pl.when(jnp.logical_and(source, jnp.logical_not(late)))
+    def _():
+        @pl.loop(1, 2 * levels)
+        def _(step):
+            @pl.when(lax.rem(z + step, 2 * levels) < levels)
+            def _():
+                a_copy(step, zh).start()
+
+        @pl.loop(1, levels + 1)
+        def _(distance):
+            @pl.when(z + distance >= levels)
+            def _():
+                pl.semaphore_wait(answer_column.at[z + distance - levels], 1)
+                a_copy(distance, zh).start()
+
+            @pl.when(jnp.logical_and(z < distance, distance < levels))
+            def _():
+                pl.semaphore_wait(answer_column.at[z - distance + levels], 1)
+                a_copy(2 * levels - distance, zh).start()
+
     @pl.when(source)
     def _():
-        @pl.when(jnp.logical_not(late))
-        def _():
-            pl.semaphore_wait(answer_column, levels)
-
-        @pl.loop(1, 2 * levels)
-        def _(step):
-            a_copy(step, zh).start()
-
         arecv[pl.ds(zh, 1)] = dsum[...].reshape(1, 8, 128)
+
+    def plane_sum(side):
+        @pl.loop(1, places)
+        def _(step):
+            factor_copy(side, step).wait_recv()
+
+        total = fsend[side, place].astype(jnp.float32)
+        for step in range(1, places):
+            total = total + frecv[side, step].astype(jnp.float32)
+        return total
+
+    fzsend[...] = plane_sum(1 - zh).astype(jnp.bfloat16)
+    fz_copy = pltpu.make_async_remote_copy(
+        src_ref=fzsend, dst_ref=fzrecv, send_sem=fz_sem.at[0], recv_sem=fz_sem.at[1],
+        device_id=across, device_id_type=MESH,
+    )
+
+    @pl.when(jnp.logical_not(late))
+    def _():
+        pl.semaphore_wait(answer_across, 1)
+
+    fz_copy.start()
 
     @pl.when(source)
     def _():
@@ -370,44 +410,11 @@
     bsend[...] = back.reshape(bsend.shape)
     send_all(back_copy)
 
-    def plane_sum(side):
-        @pl.loop(1, places)
-        def _(step):
-            factor_copy(side, step).wait_recv()
-
-        total = fsend[side, place].astype(jnp.float32)
-        for step in range(1, places):
-            total = total + frecv[side, step].astype(jnp.float32)
-        return total
-
-    fzsend[...] = plane_sum(1 - zh).astype(jnp.bfloat16)
-    fz_copy = pltpu.make_async_remote_copy(
-        src_ref=fzsend, dst_ref=fzrecv, send_sem=fz_sem.at[0], recv_sem=fz_sem.at[1],
-        device_id=across, device_id_type=MESH,
-    )
-
-    @pl.when(jnp.logical_not(late))
-    def _():
-        pl.semaphore_wait(answer_across, 1)
-
-    fz_copy.start()
-    here = plane_sum(zh)
-
+    here[...] = plane_sum(zh)
+    out = pltpu.make_async_copy(here, here_out, out_sem.at[0])
+    out.start()
     receive_all(back_copy)
-    for b in range(pg.shape[0] // block):
-        lot = jnp.concatenate([brecv[b * per_block + i] for i in range(per_block)], axis=1)
-        op[:, b * block:(b + 1) * block] = dot(lot, pg[b * block:(b + 1) * block, :], 1, 1)
-    out_p = pltpu.make_async_copy(op, op_out, out_sem.at[0])
-    out_p.start()
-
     fz_copy.wait_recv()
-    both = (here + fzrecv[...].astype(jnp.float32)) * (1.0 / tokens)
-    oa[...] = jnp.concatenate([both[:rows_a, :half], both[rows_a:, :half]], axis=1)
-    og[...] = both[:, half:]
-    out_a = pltpu.make_async_copy(oa, oa_out, out_sem.at[1])
-    out_g = pltpu.make_async_copy(og, og_out, out_sem.at[2])
-    out_a.start()
-    out_g.start()
 
     swap_a.wait_send()
     swap_g.wait_send()
@@ -440,9 +447,19 @@
     to_twin.wait_send()
     d_copy.wait_send()
     fz_copy.wait_send()
-    out_p.wait()
-    out_a.wait()
-    out_g.wait()
+    out.wait()
+
+
+def finish(tokens, rows_a, here, there, back, pg, oa, og, op):
+    half = here.shape[1] // 3
+    block = pg.shape[1]
+    per_block = block // back.shape[2]
+    both = (here[...] + there[...].astype(jnp.float32)) * (1.0 / tokens)
+    oa[...] = jnp.concatenate([both[:rows_a, :half], both[rows_a:, :half]], axis=1)
+    og[...] = both[:, half:]
+    for b in range(pg.shape[0] // block):
+        lot = jnp.concatenate([back[b * per_block + i] for i in range(per_block)], axis=1)
+        op[:, b * block:(b + 1) * block] = dot(lot, pg[b * block:(b + 1) * block, :], 1, 1)
 
 
 def shards(ny, nx, activations, out_grads, grad_weight, basis_a, basis_g):
@@ -461,28 +478,25 @@
     scratch = [
         vmem((2, here, block), bf16), vmem((2, here, wide), bf16), vmem((cols, rows), bf16),
         vmem((block, block), bf16), vmem((wide, block), bf16), vmem((ny, 2, block // ny // 2, block), bf16),
-        vmem((CHUNKS, cols, chunk), bf16), vmem((CHUNKS, cols, chunk), bf16),
-        vmem((CHUNKS, cols, chunk), bf16), vmem((CHUNKS, cols, chunk), bf16),
+        vmem((CHUNKS, cols, chunk), bf16), vmem((CHUNKS, cols, chunk), bf16), vmem((CHUNKS, cols, chunk), bf16),
         vmem((2, 8, 128), f32), vmem((places, 8, 128), f32), vmem((2, 8, 128), f32), vmem((8, 128), f32),
         vmem((2, 8, 128), f32), vmem((2, 8, 128), f32),
         vmem((2, places, rows_g, block + block // 2), bf16),
         vmem((2, places, rows_g, block + block // 2), bf16),
-        vmem((rows_g, block + block // 2), bf16),
-        vmem((rows_g, block + block // 2), bf16),
-        vmem((rows_a, block), f32), vmem((rows_g, block), f32), vmem((cols, rows), f32),
+        vmem((rows_g, block + block // 2), bf16), vmem((rows_g, block + block // 2), f32),
         dma((5,)), dma((2,)), dma((2,)), dma((levels,)), dma((ny,)), dma((2,)),
         dma((CHUNKS,)), dma((CHUNKS,)), dma((CHUNKS,)), dma((CHUNKS,)),
         dma((places,)), dma((places,)), dma((2,)), dma((2,)), dma((2 * levels,)), dma((2,)), dma((2,)),
-        pltpu.SemaphoreType.REGULAR, pltpu.SemaphoreType.REGULAR,
-        dma((2, places)), dma((2, places)), dma((2,)), dma((3,)),
+        pltpu.SemaphoreType.REGULAR, pltpu.SemaphoreType.REGULAR((levels,)),
+        dma((2, places)), dma((2, places)), dma((2,)), dma((1,)),
     ]
     anywhere = pl.BlockSpec(memory_space=pltpu.HBM)
-    factor_a, factor_g, precond = pl.pallas_call(
-        functools.partial(kernel, ny, nx, levels, tokens),
+    here, there, back = pl.pallas_call(
+        functools.partial(kernel, ny, nx, levels, tokens, rows_a, rows_g),
         out_shape=(
-            jax.ShapeDtypeStruct((rows_a, block), f32),
-            jax.ShapeDtypeStruct((rows_g, block), f32),
-            jax.ShapeDtypeStruct((cols, rows), f32),
+            jax.ShapeDtypeStruct((rows_g, block + block // 2), f32),
+            jax.ShapeDtypeStruct((rows_g, block + block // 2), bf16),
+            jax.ShapeDtypeStruct((CHUNKS, cols, chunk), bf16),
         ),
         in_specs=[anywhere] * 5,
         out_specs=(anywhere,) * 3,
@@ -491,6 +505,18 @@
             collective_id=0, has_side_effects=True, vmem_limit_bytes=60 * 1024 * 1024
         ),
     )(activations, out_grads, grad_weight.T, basis_a, basis_g)
+    inside = pl.BlockSpec(memory_space=pltpu.VMEM)
+    factor_a, factor_g, precond = pl.pallas_call(
+        functools.partial(finish, tokens, rows_a),
+        out_shape=(
+            jax.ShapeDtypeStruct((rows_a, block), f32),
+            jax.ShapeDtypeStruct((rows_g, block), f32),
+            jax.ShapeDtypeStruct((cols, rows), f32),
+        ),
+        in_specs=[inside] * 4,
+        out_specs=(inside,) * 3,
+        compiler_params=pltpu.CompilerParams(vmem_limit_bytes=60 * 1024 * 1024),
+    )(here, there, back, basis_g)
     return factor_a, factor_g, precond.T
 
 

time: 53.2 us -> 47.9 us (0.900)
  the two profiles are of different devices: /device:TPU:5 before, /device:TPU:1 now
where the time goes in v3:
time: 47.9 us; the launch traced here: 47.1 us
  Pallas kernels  46.5 us (97%)
  between operations  0.64 us (1%)
    pallas_call x1, Pallas kernels, shards(): pl.pallas_call(functools.partial(kernel, ny, nx, levels, tokens, rows_a,...  44 us
    pallas_call x1, Pallas kernels, shards(): pl.pallas_call(functools.partial(finish, tokens, rows_a), out_shape=(jax....  2.49 us

profile of v3, /device:TPU:1, one launch (start us, length us, event | category | flops | bytes accessed | tf_op | source)
XLA Modules:
  0.0 47.1 jit_solution(3325883284587453802)
XLA Ops:
  0.6 44.0 %shard_map.76 = (f32[16,768]{1,0:T(8,128)}, bf16[16,768]{1,0:T(8,128)(2,1)}, bf16[8,64,128]{2,1,0:T(8,128)(2,1)}) custom-call(bf16[128,512]{1,0:T(8,128)(2,1)} %xa_in.1, bf16[128,1024]{1,0:T(8,128)(2,1)} %xg_in.1, bf16[64,1024]{1,0:T(8,128)(2,1)} %bitcast.2, bf16[512,512]{1,0:T(8,128)(2,1)} %qa_in.1, bf16[1024,512]{1,0:T(8,128)(2,1)} %pg.1), custom_call_target="tpu_custom_call" | custom-call | tf_op jit(solution)/shard_map/pallas_call | solution.py:494
  44.6 2.5 %shard_map.77 = (f32[8,512]{1,0:T(8,128)}, f32[16,512]{1,0:T(8,128)}, f32[64,1024]{1,0:T(8,128)}) custom-call(f32[16,768]{1,0:T(8,128)} %get-tuple-element.9.here, bf16[16,768]{1,0:T(8,128)(2,1)} %get-tuple-element.10.there, bf16[8,64,128]{2,1,0:T(8,128)(2,1)} %get-tuple-element.11.back, bf16[1024,512]{1,0:T(8,128)(2,1)} %pg.1), custom_call_target="tpu_custom_call" | custom-call | tf_op jit(solution)/shard_map/pallas_call | solution.py:509

commit v4 on v3

--- a/solution.py
+++ b/solution.py
@@ -176,6 +176,66 @@
             device_id=at_place(to), device_id_type=MESH,
         )
 
+    part = block // ny // 2
+
+    def q_copy(step, from_y):
+        return pltpu.make_async_remote_copy(
+            src_ref=qa.at[pl.ds(pl.multiple_of((y * 2 + core) * part, 16), part)],
+            dst_ref=qj.at[from_y, core],
+            send_sem=q_send.at[step], recv_sem=q_recv.at[from_y],
+            device_id=at_yz(given_y, z + step + 1 - odd - reach), device_id_type=MESH,
+        )
+
+    def q_is_own(step):
+        return jnp.logical_and(source, step + 1 - odd == reach)
+
+    @pl.when(gives)
+    def _():
+        @pl.loop(0, levels)
+        def _(turn):
+            step = jnp.where(lax.rem(turn, 2) == 0, levels - 1 - turn // 2, turn // 2)
+
+            @pl.when(jnp.logical_not(q_is_own(step)))
+            def _():
+                q_copy(step, y).start()
+
+    def to_twin(from_y, core_side):
+        return pltpu.make_async_remote_copy(
+            src_ref=qj.at[from_y, core_side], dst_ref=qj.at[from_y, core_side],
+            send_sem=twin_sem.at[0, from_y], recv_sem=twin_sem.at[1, from_y],
+            device_id=twin, device_id_type=MESH,
+        )
+
+    def left_copy(q, slot):
+        return pltpu.make_async_remote_copy(
+            src_ref=lsend.at[q], dst_ref=lrecv.at[slot],
+            send_sem=lsend_sem.at[q], recv_sem=lrecv_sem.at[slot],
+            device_id=friend(q), device_id_type=MESH,
+        )
+
+    def back_copy(q, slot):
+        return pltpu.make_async_remote_copy(
+            src_ref=bsend.at[q], dst_ref=brecv.at[slot],
+            send_sem=bsend_sem.at[q], recv_sem=brecv_sem.at[slot],
+            device_id=friend(q), device_id_type=MESH,
+        )
+
+    def send_all(copy):
+        @pl.loop(0, CHUNKS)
+        def _(q):
+            copy(q, lane).start()
+
+    def receive_all(copy):
+        @pl.loop(0, CHUNKS)
+        def _(k):
+            copy(k, k).wait_recv()
+
+    def drain_all(copy):
+        @pl.loop(0, CHUNKS)
+        def _(q):
+            copy(q, lane).wait_send()
+
+
     @pl.loop(1, places)
     def _(step):
         diag_copy(step).start()
@@ -190,63 +250,6 @@
     )
     swap_a.start()
     swap_g.start()
-
-    part = block // ny // 2
-
-    def q_copy(step, from_y):
-        return pltpu.make_async_remote_copy(
-            src_ref=qa.at[pl.ds(pl.multiple_of((y * 2 + core) * part, 16), part)],
-            dst_ref=qj.at[from_y, core],
-            send_sem=q_send.at[step], recv_sem=q_recv.at[from_y],
-            device_id=at_yz(given_y, z + step + 1 - odd - reach), device_id_type=MESH,
-        )
-
-    def q_is_own(step):
-        return jnp.logical_and(source, step + 1 - odd == reach)
-
-    @pl.when(gives)
-    def _():
-        @pl.loop(0, levels)
-        def _(step):
-            @pl.when(jnp.logical_not(q_is_own(step)))
-            def _():
-                q_copy(step, y).start()
-
-    to_twin = pltpu.make_async_remote_copy(
-        src_ref=qj.at[:, core], dst_ref=qj.at[:, core],
-        send_sem=twin_sem.at[0], recv_sem=twin_sem.at[1],
-        device_id=twin, device_id_type=MESH,
-    )
-
-    def left_copy(q, slot):
-        return pltpu.make_async_remote_copy(
-            src_ref=lsend.at[q], dst_ref=lrecv.at[slot],
-            send_sem=lsend_sem.at[q], recv_sem=lrecv_sem.at[slot],
-            device_id=friend(q), device_id_type=MESH,
-        )
-
-    def back_copy(q, slot):
-        return pltpu.make_async_remote_copy(
-            src_ref=bsend.at[q], dst_ref=brecv.at[slot],
-            send_sem=bsend_sem.at[q], recv_sem=brecv_sem.at[slot],
-            device_id=friend(q), device_id_type=MESH,
-        )
-
-    def send_all(copy):
-        @pl.loop(0, CHUNKS)
-        def _(q):
-            copy(q, lane).start()
-
-    def receive_all(copy):
-        @pl.loop(0, CHUNKS)
-        def _(k):
-            copy(k, k).wait_recv()
-
-    def drain_all(copy):
-        @pl.loop(0, CHUNKS)
-        def _(q):
-            copy(q, lane).wait_send()
-
 
     swap_a.wait_recv()
     swap_g.wait_recv()
@@ -378,11 +381,12 @@
         def _():
             q_copy(0, from_y).wait_recv()
 
-    to_twin.start()
+        to_twin(from_y, core).start()
 
     receive_all(left_copy)
     rows = lrecv.shape[2]
-    to_twin.wait_recv()
+    for from_y in range(ny):
+        to_twin(from_y, 1 - core).wait_recv()
     rotated = dot(lrecv[...].reshape(block, rows), qj[...].reshape(block, block), 0, 0)
 
     @pl.when(source)
@@ -413,13 +417,9 @@
     here[...] = plane_sum(zh)
     out = pltpu.make_async_copy(here, here_out, out_sem.at[0])
     out.start()
-    receive_all(back_copy)
-    fz_copy.wait_recv()
-
     swap_a.wait_send()
     swap_g.wait_send()
     drain_all(left_copy)
-    drain_all(back_copy)
 
     @pl.loop(1, places)
     def _(step):
@@ -444,10 +444,17 @@
             def _():
                 q_copy(step, y).wait_send()
 
-    to_twin.wait_send()
+    for from_y in range(ny):
+        to_twin(from_y, core).wait_send()
+
     d_copy.wait_send()
     fz_copy.wait_send()
     out.wait()
+
+    receive_all(back_copy)
+    fz_copy.wait_recv()
+
+    drain_all(back_copy)
 
 
 def finish(tokens, rows_a, here, there, back, pg, oa, og, op):
@@ -484,7 +491,7 @@
         vmem((2, places, rows_g, block + block // 2), bf16),
         vmem((2, places, rows_g, block + block // 2), bf16),
         vmem((rows_g, block + block // 2), bf16), vmem((rows_g, block + block // 2), f32),
-        dma((5,)), dma((2,)), dma((2,)), dma((levels,)), dma((ny,)), dma((2,)),
+        dma((5,)), dma((2,)), dma((2,)), dma((levels,)), dma((ny,)), dma((2, ny)),
         dma((CHUNKS,)), dma((CHUNKS,)), dma((CHUNKS,)), dma((CHUNKS,)),
         dma((places,)), dma((places,)), dma((2,)), dma((2,)), dma((2 * levels,)), dma((2,)), dma((2,)),
         pltpu.SemaphoreType.REGULAR, pltpu.SemaphoreType.REGULAR((levels,)),

time: 47.9 us -> 46.9 us (0.979); the launches traced: 47.1 us -> 46.7 us
  no operation moved by 1% of the time
where the time goes in v4:
time: 46.9 us; the launch traced here: 46.7 us
  Pallas kernels  46.1 us (98%)
  between operations  0.64 us (1%)
    pallas_call x1, Pallas kernels, shards(): pl.pallas_call(functools.partial(kernel, ny, nx, levels, tokens, rows_a,...  43.6 us
    pallas_call x1, Pallas kernels, shards(): pl.pallas_call(functools.partial(finish, tokens, rows_a), out_shape=(jax....  2.49 us

profile of v4, /device:TPU:1, one launch (start us, length us, event | category | flops | bytes accessed | tf_op | source)
XLA Modules:
  0.0 46.7 jit_solution(12385742951815959370)
XLA Ops:
  0.6 43.6 %shard_map.76 = (f32[16,768]{1,0:T(8,128)}, bf16[16,768]{1,0:T(8,128)(2,1)}, bf16[8,64,128]{2,1,0:T(8,128)(2,1)}) custom-call(bf16[128,512]{1,0:T(8,128)(2,1)} %xa_in.1, bf16[128,1024]{1,0:T(8,128)(2,1)} %xg_in.1, bf16[64,1024]{1,0:T(8,128)(2,1)} %bitcast.2, bf16[512,512]{1,0:T(8,128)(2,1)} %qa_in.1, bf16[1024,512]{1,0:T(8,128)(2,1)} %pg.1), custom_call_target="tpu_custom_call" | custom-call | tf_op jit(solution)/shard_map/pallas_call | solution.py:501
  44.2 2.5 %shard_map.77 = (f32[8,512]{1,0:T(8,128)}, f32[16,512]{1,0:T(8,128)}, f32[64,1024]{1,0:T(8,128)}) custom-call(f32[16,768]{1,0:T(8,128)} %get-tuple-element.9.here, bf16[16,768]{1,0:T(8,128)(2,1)} %get-tuple-element.10.there, bf16[8,64,128]{2,1,0:T(8,128)(2,1)} %get-tuple-element.11.back, bf16[1024,512]{1,0:T(8,128)(2,1)} %pg.1), custom_call_target="tpu_custom_call" | custom-call | tf_op jit(solution)/shard_map/pallas_call | solution.py:516

commit v5 on v4

--- a/solution.py
+++ b/solution.py
@@ -412,7 +412,10 @@
     scaled = (rotated / (diag_g * diag_a + damping)).astype(jnp.bfloat16)
     back = dot(qj[...].reshape(block, block), scaled, 1, 1).astype(jnp.bfloat16)
     bsend[...] = back.reshape(bsend.shape)
-    send_all(back_copy)
+    for side in range(2):
+        for q in range(CHUNKS):
+            if q // 2 % 2 == side:
+                back_copy(q, lane).start()
 
     here[...] = plane_sum(zh)
     out = pltpu.make_async_copy(here, here_out, out_sem.at[0])

time: 46.9 us -> 46.9 us (level)
  no operation moved by 1% of the time
where the time goes in v5:
time: 46.9 us; the launch traced here: 46.7 us
  Pallas kernels  46.1 us (98%)
  between operations  0.64 us (1%)
    pallas_call x1, Pallas kernels, shards(): pl.pallas_call(functools.partial(kernel, ny, nx, levels, tokens, rows_a,...  43.6 us
    pallas_call x1, Pallas kernels, shards(): pl.pallas_call(functools.partial(finish, tokens, rows_a), out_shape=(jax....  2.49 us

profile of v5, /device:TPU:1, one launch (start us, length us, event | category | flops | bytes accessed | tf_op | source)
XLA Modules:
  0.0 46.7 jit_solution(315308068960884694)
XLA Ops:
  0.6 43.6 %shard_map.76 = (f32[16,768]{1,0:T(8,128)}, bf16[16,768]{1,0:T(8,128)(2,1)}, bf16[8,64,128]{2,1,0:T(8,128)(2,1)}) custom-call(bf16[128,512]{1,0:T(8,128)(2,1)} %xa_in.1, bf16[128,1024]{1,0:T(8,128)(2,1)} %xg_in.1, bf16[64,1024]{1,0:T(8,128)(2,1)} %bitcast.2, bf16[512,512]{1,0:T(8,128)(2,1)} %qa_in.1, bf16[1024,512]{1,0:T(8,128)(2,1)} %pg.1), custom_call_target="tpu_custom_call" | custom-call | tf_op jit(solution)/shard_map/pallas_call | solution.py:504
  44.2 2.5 %shard_map.77 = (f32[8,512]{1,0:T(8,128)}, f32[16,512]{1,0:T(8,128)}, f32[64,1024]{1,0:T(8,128)}) custom-call(f32[16,768]{1,0:T(8,128)} %get-tuple-element.9.here, bf16[16,768]{1,0:T(8,128)(2,1)} %get-tuple-element.10.there, bf16[8,64,128]{2,1,0:T(8,128)(2,1)} %get-tuple-element.11.back, bf16[1024,512]{1,0:T(8,128)(2,1)} %pg.1), custom_call_target="tpu_custom_call" | custom-call | tf_op jit(solution)/shard_map/pallas_call | solution.py:519
